TPU v7x, 32 devices: a whole 2x2x4 slice. The times are simulated.
32 devices in a mesh: group: 8 (over z, y), tensor: 4 (over x, core).
Axes of the slice: x: 2, y: 2, z: 4, core: 2. Of those that a mesh axis runs over, the one named last changes fastest.
Arguments:
- query: bfloat16 [2, 256, 2048], P(None, 'group', 'tensor'), may hold values from -80 to 80
- self_kv: bfloat16 [2, 256, 2, 2048], P(None, 'group', None, 'tensor'), may hold values from -6 to 6
- kv_pages: bfloat16 [2, 384, 16, 2, 2048], P(None, 'group', None, None, 'tensor'), may hold values from -6 to 6
- page_dest: int32 [384, 1], replicated, may hold values from 0 to 7; in each aligned block of 48 rows (0 to 47, 48 to 95, ...) at most 12 rows name the same one
- page_request: int32 [384], replicated, may hold values from 0 to 1
- score_len: int32 [16], P('group'), may hold values from 1 to 16
- out_proj: bfloat16 [2, 2048, 2048], P(None, 'tensor'), may hold values from -0.125 to 0.125
- residual: bfloat16 [2, 256, 2048], P(None, ('group', 'tensor')), may hold values from -6 to 6
- norm_gain: float32 [2, 2048], replicated, may hold values from 0.5 to 40
- norm_bias: float32 [2, 2048], replicated, may hold values from -3 to 3
- vocab: bfloat16 [2, 2048, 24576], P(None, None, ('group', 'tensor')), may hold values from -0.3984375 to 0.3984375
- targets: int32 [256], replicated, may hold values from 0 to 24575
Outputs:
- logprob: float32 [2, 256], P(None, ('group', 'tensor'))
Inputs may be any that keep to these rules, and one draw needn't show every extreme that they name: `page_dest`: the 48 pages of each aligned block (pages held by one group) go to any one group at most 12 times; some block sends exactly 12 to some group.
All inputs are finite; a program needn't handle non-finite values.
Results may differ from a plain program's by a relative error of at most 0.00097.
Values may be sent and summed in bfloat16 or wider, within the bound.
A program may use at most 192 MiB of HBM per device.

v0:
```python
import math

import jax
import jax.numpy as jnp
from jax import lax
from jax.sharding import PartitionSpec as P

HEADS = 16
HEAD_DIM = 128
REQ_GRP = 2
SCORE_LEN = 16


NEGATIVE = -1e30
EPSILON = 1e-05


def route_tables(destination, request, groups, per_owner, capacity, requests):
    page_count = destination.shape[0]
    owner_group = jnp.arange(page_count, dtype=jnp.int32) // per_owner
    columns = jnp.arange(groups, dtype=jnp.int32)
    onehot = (destination[:, None] == columns[None, :]).astype(jnp.int32)
    within = jnp.cumsum(onehot.reshape(groups, per_owner, groups), axis=1).reshape(
        page_count, groups
    )
    position = jnp.sum(within * onehot, axis=1) - 1
    arrival = owner_group * capacity + position
    combined = destination * requests + request
    pair_hot = (
        combined[:, None] == jnp.arange(groups * requests, dtype=jnp.int32)[None, :]
    ).astype(jnp.int32)
    running = jnp.cumsum(pair_hot, axis=0)
    page_rank = jnp.sum(running * pair_hot, axis=1) - 1
    totals = running[-1].reshape(groups, requests)
    return (position, arrival, page_rank, totals)


def alibi_slopes(head_count):
    return jnp.exp2(-8.0 * jnp.arange(1, head_count + 1).astype(jnp.float32) / head_count)


def per_device(
    query,
    self_kv,
    kv_pages,
    page_dest,
    page_request,
    score_len,
    out_proj,
    residual,
    norm_gain,
    norm_bias,
    vocab,
    targets,
):
    groups = lax.axis_size("group")
    shards = lax.axis_size("tensor")
    group_id = lax.axis_index("group")
    tensor_id = lax.axis_index("tensor")
    tok_grp = query.shape[1]
    flat_width = query.shape[2]
    head_local = flat_width // HEAD_DIM
    per_owner = kv_pages.shape[1]
    page_len = kv_pages.shape[2]
    capacity = 2 * per_owner // groups
    destination = page_dest[:, 0]
    page_total = destination.shape[0]
    position, arrival, page_rank, totals = route_tables(
        destination, page_request, groups, per_owner, capacity, REQ_GRP
    )
    slopes = lax.dynamic_slice_in_dim(alibi_slopes(HEADS), tensor_id * head_local, head_local)
    score_scale = 1.0 / math.sqrt(HEAD_DIM)
    queries = query.reshape(2, tok_grp, head_local, HEAD_DIM)
    own_keys = self_kv[:, :, 0].reshape(2, tok_grp, head_local, HEAD_DIM)
    own_values = self_kv[:, :, 1].reshape(2, tok_grp, head_local, HEAD_DIM)
    token_ids = jnp.arange(tok_grp, dtype=jnp.int32)
    token_request = token_ids // SCORE_LEN
    token_step = token_ids % SCORE_LEN
    own_distance = (token_step[:, None] - token_step[None, :]).astype(jnp.float32)
    own_scores = (
        jnp.einsum("mthd,mshd->mhts", queries, own_keys, preferred_element_type=jnp.float32)
        * score_scale
    )
    own_scores = own_scores - slopes[None, :, None, None] * own_distance[None, None]
    own_allowed = (
        (token_request[:, None] == token_request[None, :])
        & (token_step[None, :] <= token_step[:, None])
    )[None, None]
    own_scores = jnp.where(own_allowed, own_scores, NEGATIVE)
    own_top = jnp.max(own_scores, -1)
    my_dest = lax.dynamic_slice_in_dim(destination, group_id * per_owner, per_owner)
    my_position = lax.dynamic_slice_in_dim(position, group_id * per_owner, per_owner)
    buffer = groups * capacity
    outgoing = jnp.zeros((2, buffer, page_len, 2, flat_width), jnp.bfloat16)
    outgoing = outgoing.at[:, my_dest * capacity + my_position].set(kv_pages)
    incoming = lax.all_to_all(outgoing, "group", split_axis=1, concat_axis=1, tiled=True)
    target_place = jnp.where(destination == group_id, arrival, buffer)
    slot_index = (
        jnp.full((buffer,), page_total, jnp.int32)
        .at[target_place]
        .set(jnp.arange(page_total, dtype=jnp.int32), mode="drop")
    )
    is_valid = slot_index < page_total
    safe_index = jnp.minimum(slot_index, page_total - 1)
    key_data = incoming[:, :, :, 0].reshape(2, buffer * page_len, head_local, HEAD_DIM)
    values = incoming[:, :, :, 1].reshape(2, buffer * page_len, head_local, HEAD_DIM)
    key_request = jnp.repeat(jnp.where(is_valid, page_request[safe_index], -1), page_len)
    key_position = (
        page_rank[safe_index][:, None] * page_len + jnp.arange(page_len, dtype=jnp.int32)[None, :]
    ).reshape(-1)
    context = totals[group_id][token_request] * page_len
    distance = ((context + token_step)[:, None] - key_position[None, :]).astype(jnp.float32)
    scores = (
        jnp.einsum("mthd,mkhd->mhtk", queries, key_data, preferred_element_type=jnp.float32)
        * score_scale
    )
    scores = scores - slopes[None, :, None, None] * distance[None, None]
    allowed = (key_request[None, :] == token_request[:, None])[None, None]
    scores = jnp.where(allowed, scores, NEGATIVE)
    row_top = jnp.maximum(jnp.max(scores, -1), own_top)
    exp_terms = jnp.where(allowed, jnp.exp(scores - row_top[..., None]), 0.0)
    denominator = jnp.sum(exp_terms, -1)
    numerator = jnp.einsum(
        "mhtk,mkhd->mthd",
        exp_terms.astype(jnp.bfloat16),
        values,
        preferred_element_type=jnp.float32,
    )
    own_terms = jnp.where(own_allowed, jnp.exp(own_scores - row_top[..., None]), 0.0)
    denominator = denominator + jnp.sum(own_terms, -1)
    numerator = numerator + jnp.einsum(
        "mhts,mshd->mthd",
        own_terms.astype(jnp.bfloat16),
        own_values,
        preferred_element_type=jnp.float32,
    )
    attended = (
        (numerator / jnp.transpose(denominator, (0, 2, 1))[..., None])
        .reshape(2, tok_grp, flat_width)
        .astype(jnp.bfloat16)
    )
    rows_local = tok_grp // shards
    mixed = lax.psum_scatter(
        jnp.einsum("mtk,mkd->tmd", attended, out_proj, preferred_element_type=jnp.float32),
        "tensor",
        scatter_dimension=0,
        tiled=True,
    )
    hidden = residual.astype(jnp.float32) + jnp.transpose(mixed, (1, 0, 2))
    row_mean = jnp.mean(hidden, axis=-1, keepdims=True)
    centered = hidden - row_mean
    variance = jnp.mean(centered * centered, axis=-1, keepdims=True)
    normed = (
        centered / jnp.sqrt(variance + EPSILON) * norm_gain[:, None, :] + norm_bias[:, None, :]
    ).astype(jnp.bfloat16)
    voc_local = vocab.shape[2]
    offset = (group_id * shards + tensor_id) * voc_local
    logits = jnp.einsum(
        "mnd,mdv->mnv",
        lax.all_gather(normed, ("group", "tensor"), axis=1, tiled=True),
        vocab,
        preferred_element_type=jnp.float32,
    )
    row_peak = lax.pmax(jnp.max(logits, axis=2), ("group", "tensor"))
    wanted = targets - offset
    inside = (wanted >= 0) & (wanted < voc_local)
    picked = jnp.take_along_axis(logits, jnp.clip(wanted, 0, voc_local - 1)[None, :, None], axis=2)[
        ..., 0
    ]
    exp_total, chosen = lax.psum(
        (
            jnp.sum(jnp.exp(logits - row_peak[..., None]), axis=2),
            jnp.where(inside[None, :], picked, 0.0),
        ),
        ("group", "tensor"),
    )
    logprob_all = chosen - (row_peak + jnp.log(exp_total))
    mine = lax.dynamic_slice_in_dim(
        logprob_all, group_id * tok_grp + tensor_id * rows_local, rows_local, 1
    )
    local_ids = tensor_id * rows_local + jnp.arange(rows_local, dtype=jnp.int32)
    keep_token = local_ids % SCORE_LEN < score_len[local_ids // SCORE_LEN]
    return jnp.where(keep_token[None, :], mine, 0.0)


def solution(mesh):
    in_specs = (
        P(None, "group", "tensor"),
        P(None, "group", None, "tensor"),
        P(None, "group", None, None, "tensor"),
        P(),
        P(),
        P("group"),
        P(None, "tensor", None),
        P(None, ("group", "tensor"), None),
        P(),
        P(),
        P(None, None, ("group", "tensor")),
        P(),
    )
    out_specs = P(None, ("group", "tensor"))
    return jax.shard_map(
        per_device, mesh=mesh, in_specs=in_specs, out_specs=out_specs, check_vma=False
    )
```

profile of v0, /device:TPU:0, one launch (start us, length us, event | category | flops | bytes accessed | tf_op | source)
XLA Modules:
  0.0 425.7 jit_solution(11296668252917291768)
XLA Ops:
  6.5 0.7 reduce.1
  7.4 1.0 fusion.73
  8.6 2.7 copy.77
  11.5 3.5 broadcast_in_dim.127
  14.9 7.9 %scatter_fusion = bf16[2,96,16,2,512]{4,2,3,1,0:T(8,128)(2,1)} fusion(bf16[2,96,16,2,512]{4,2,3,1,0:T(8,128)(2,1)} %broadcast_in_dim.127, s32[48]{0:T(128)S(1)} %compare_select_fusion.5, bf16[48,2,16,2,512]{4,2,3,1,0:T(8,128)(2,1)S(1)} %copy.77), kind=kCustom, calls=%fused_computation.4 | custom fusion | bytes 9437376 | tf_op jit(solution)/shard_map/scatter | solution.py:95
  22.8 6.8 %copy.78 = bf16[2,96,16,2,512]{4,2,3,0,1:T(8,128)(2,1)} copy(bf16[2,96,16,2,512]{4,2,3,1,0:T(8,128)(2,1)} %scatter_fusion) | data formatting | bytes 12582912 | tf_op jit(solution)/shard_map/scatter | solution.py:95
  29.6 7.4 %all-to-all-start = ((bf16[2,96,16,2,512]{4,2,3,0,1:T(8,128)(2,1)}), bf16[2,96,16,2,512]{4,2,3,0,1:T(8,128)(2,1)}, u32[]{:S(2)}, u32[]{:S(2)}) async-start(bf16[2,96,16,2,512]{4,2,3,0,1:T(8,128)(2,1)} %copy.78), calls=%async_computation | async-start | bytes 12582912 | tf_op jit(solution)/shard_map/all_to_all | solution.py:96
  37.2 0.9 reduce-window.6
  38.7 2.9 scatter_custom_fusion.1
  41.6 1.3 gather_fusion.1
  43.0 1.3 gather_fusion.2
  45.3 1.3 fusion.61
  47.8 1.1 broadcast_multiply_fusion
  48.8 126.4 %all-to-all-done = bf16[2,96,16,2,512]{4,2,3,0,1:T(8,128)(2,1)} async-done(((bf16[2,96,16,2,512]{4,2,3,0,1:T(8,128)(2,1)}), bf16[2,96,16,2,512]{4,2,3,0,1:T(8,128)(2,1)}, u32[]{:S(2)}, u32[]{:S(2)}) %all-to-all-start) | async-done | bytes 6291488 | tf_op jit(solution)/shard_map/all_to_all | solution.py:96
  175.2 5.6 %fusion.71 = (bf16[2,96,16,1,512]{4,2,3,0,1:T(8,128)(2,1)S(1)}, bf16[2,96,16,1,512]{4,2,3,0,1:T(8,128)(2,1)}) fusion(bf16[2,96,16,2,512]{4,2,3,0,1:T(8,128)(2,1)} %all-to-all-done), kind=kLoop, calls=%fused_computation.142 | loop fusion | bytes 12582912 | tf_op jit(solution)/shard_map/slice | solution.py:105
  181.3 3.0 reshape_squeeze.16
  184.3 3.5 fusion.74
  188.3 0.6 copy-done.5
  189.3 3.0 reshape_squeeze.15
  192.4 3.3 fusion.22
  196.0 1.6 convolution_bitcast_fusion
  197.9 20.6 %reduce-scatter.2.cloned.1.call-done = f32[8,2,2048]{2,0,1:T(8,128)} async-done(((f32[32,2,2048]{2,0,1:T(8,128)}), f32[8,2,2048]{2,0,1:T(8,128)}) %reduce-scatter.2.cloned.1.call-update) | async-done | bytes 131088 | tf_op jit(solution)/shard_map/reduce_scatter | solution.py:143
  218.5 1.0 fusion.49
  219.5 1.1 multiply_reduce_fusion
  220.6 1.6 add_convert_fusion
  223.0 55.8 %all-gather.2.cloned.1.call-done = bf16[2,256,2048]{2,1,0:T(8,128)(2,1)} async-done(((bf16[2,8,2048]{2,1,0:T(8,128)(2,1)}), bf16[2,256,2048]{2,1,0:T(8,128)(2,1)}) %all-gather.2.cloned.1.call-update) | async-done | bytes 2097168 | tf_op jit(solution)/shard_map/all_gather | solution.py:160
  278.9 5.3 %fusion.76 = (f32[2,256]{1,0:T(2,128)S(1)}, f32[2,256,768]{2,1,0:T(8,128)S(1)}) fusion(bf16[2,256,2048]{2,1,0:T(8,128)(2,1)} %all-gather.2.cloned.1.call-done, bf16[2,2048,768]{2,1,0:T(8,128)(2,1)} %param.22), kind=kOutput, calls=%fused_computation.147 | convolution fusion | flops 1611005440 | bytes 9963520 | tf_op jit(solution)/shard_map/mnd,mdv->mnv/dot_general | solution.py:158
  284.1 47.6 %copy.90 = f32[2,256,768]{0,2,1:T(8,128)} copy(f32[2,256,768]{2,1,0:T(8,128)S(1)} %get-tuple-element.23) | data formatting | bytes 3145728 | tf_op jit(solution)/shard_map/mnd,mdv->mnv/dot_general | solution.py:158
  331.9 39.5 %pmax.7 = f32[2,256]{0,1:T(8,128)S(1)} all-reduce(f32[2,256]{0,1:T(8,128)S(1)} %copy.91), channel_id=1, replica_groups=mesh['group'=8,'tensor'=4] {'group','tensor'}, use_global_device_ids=true, to_apply=%region_16.17 | all-reduce | flops 512 | bytes 4096 | tf_op jit(solution)/shard_map/pmax | solution.py:164
  372.1 2.3 gather_fusion.3
  374.6 43.5 %all-reduce = (f32[2,256]{0,1:T(8,128)S(1)}, f32[2,256]{0,1:T(8,128)S(1)}) all-reduce(f32[2,256]{0,1:T(8,128)S(1)} %select_bitcast_fusion, f32[2,256]{0,1:T(8,128)S(1)} %copy.93), channel_id=1, replica_groups=mesh['group'=8,'tensor'=4] {'group','tensor'}, use_global_device_ids=true, to_apply=%region_14.15 | all-reduce | flops 1024 | bytes 8192 | tf_op jit(solution)/shard_map/psum | solution.py:170
  418.2 0.6 copy.94
  (88 shorter events, 6.9 us)
Async XLA Ops:
  6.5 40.8 %copy-start = (bf16[2,32,512]{2,1,0:T(8,128)(2,1)S(1)}, bf16[2,32,512]{2,1,0:T(8,128)(2,1)}, u32[]{:S(2)}) copy-start(bf16[2,32,512]{2,1,0:T(8,128)(2,1)} %param.12) | copy-start | bytes 196612
  8.6 2.8 copy-start.10
  29.6 7.6 %copy-start.2 = (s32[384]{0:T(512)S(1)}, s32[384]{0:T(512)}, u32[]{:S(2)}) copy-start(s32[384]{0:T(512)} %param.16) | copy-start | bytes 4612
  29.6 17.0 %copy-start.7 = (bf16[2,32,2,512]{3,2,1,0:T(2,128)(2,1)S(1)}, bf16[2,32,2,512]{3,2,1,0:T(2,128)(2,1)}, u32[]{:S(2)}) copy-start(bf16[2,32,2,512]{3,2,1,0:T(2,128)(2,1)} %param.13) | copy-start | bytes 393220
  29.6 145.6 %all-to-all-start = ((bf16[2,96,16,2,512]{4,2,3,0,1:T(8,128)(2,1)}), bf16[2,96,16,2,512]{4,2,3,0,1:T(8,128)(2,1)}, u32[]{:S(2)}, u32[]{:S(2)}) async-start(bf16[2,96,16,2,512]{4,2,3,0,1:T(8,128)(2,1)} %copy.78), calls=%async_computation | async-start | bytes 12582912 | tf_op jit(solution)/shard_map/all_to_all | solution.py:96
  37.0 181.4 %reduce-scatter.2.cloned.1.call-start = ((), (), s32[]{:S(2)}) async-start(), calls=%async_computation.2 | async-start | bytes 655360 | tf_op jit(solution)/shard_map/reduce_scatter | solution.py:143
  184.3 4.7 %copy-start.3 = (bf16[2,96,16,1,512]{4,2,3,0,1:T(8,128)(2,1)S(1)}, bf16[2,96,16,1,512]{4,2,3,0,1:T(8,128)(2,1)}, u32[]{:S(2)}) copy-start(bf16[2,96,16,1,512]{4,2,3,0,1:T(8,128)(2,1)} %get-tuple-element.14) | copy-start | bytes 9437188
  187.8 1.1 copy-start.5
  192.3 3.6 copy-start.4
  195.6 22.8 %copy-start.6 = (bf16[2,8,2048]{2,1,0:T(8,128)(2,1)S(1)}, bf16[2,8,2048]{2,1,0:T(8,128)(2,1)}, u32[]{:S(2)}) copy-start(bf16[2,8,2048]{2,1,0:T(8,128)(2,1)} %param.19) | copy-start | bytes 196612
  196.0 24.6 %copy-start.8 = (f32[2,2048]{1,0:T(2,128)S(1)}, f32[2,2048]{1,0:T(2,128)}, u32[]{:S(2)}) copy-start(f32[2,2048]{1,0:T(2,128)} %param.21) | copy-start | bytes 49156
  196.0 24.6 %copy-start.9 = (f32[2,2048]{1,0:T(2,128)S(1)}, f32[2,2048]{1,0:T(2,128)}, u32[]{:S(2)}) copy-start(f32[2,2048]{1,0:T(2,128)} %param.20) | copy-start | bytes 49156
  196.0 26.3 %copy-start.1 = (s32[2]{0:T(128)S(1)}, s32[2]{0:T(128)}, u32[]{:S(2)}) copy-start(s32[2]{0:T(128)} %param.17) | copy-start | bytes 28
  196.0 27.0 %copy-start.11 = (s32[256]{0:T(256)S(1)}, s32[256]{0:T(256)}, u32[]{:S(2)}) copy-start(s32[256]{0:T(256)} %param.23) | copy-start | bytes 3076
  197.6 81.2 %all-gather.2.cloned.1.call-start = ((), (), s32[]{:S(2)}) async-start(), calls=%async_computation.3 | async-start | bytes 2162688 | tf_op jit(solution)/shard_map/all_gather | solution.py:160
Sparse Core Ops, SparseCore 0:
  197.7 20.6 reduce-scatter.1
  222.4 56.4 all-gather.1
where the time goes:
time: 426 us
  waiting for transfers between devices  203 us (48%)
  local copies, waits for them, and re-layouts  93.4 us (22%)
  blocking collectives  83 us (19%)
  matrix products  14.1 us (3%)
  between operations  13.8 us (3%)
  other arithmetic  10.7 us (3%)
  starting transfers between devices  7.67 us (2%)
    all_to_all x1, waiting for transfers between devices, per_device(): lax.all_to_all(outgoing, 'group', split_axis=1, concat_axis=1, tiled=True)  126 us
    all_gather x1, waiting for transfers between devices, per_device(): lax.all_gather(normed, ('group', 'tensor'), axis=1, tiled=True)  55.8 us
    dot_general x1, local copies, waits for them, and re-layouts, per_device(): jnp.einsum('mnd,mdv->mnv', lax.all_gather(normed, ('group', 'tensor'), ax...  47.6 us
    psum x1, blocking collectives, per_device(): lax.psum((jnp.sum(jnp.exp(logits - row_peak[..., None]), axis=2), jnp.whe...  43.5 us
    pmax x1, blocking collectives, per_device(): row_peak = lax.pmax(jnp.max(logits, axis=2), ('group', 'tensor'))  39.5 us
    reduce_scatter x1, waiting for transfers between devices, per_device(): lax.psum_scatter(jnp.einsum('mtk,mkd->tmd', attended, out_proj, preferred...  20.6 us
    scatter x2, local copies, waits for them, and re-layouts, per_device(): outgoing = outgoing.at[:, my_dest * capacity + my_position].set(kv_pages)  14.7 us
  transfers between devices with their start and end apart: 3, of which 3 were waited for; matrix products, arithmetic and copies ran while one was open for 3% of the time, Pallas kernels for 0%

commit v1 on v0

v1 whole, which is shorter than its diff:
```python
import functools
import math

import jax
import jax.numpy as jnp
from jax import lax
from jax.experimental import pallas as pl
from jax.experimental.pallas import tpu as pltpu
from jax.sharding import PartitionSpec as P

HEADS = 16
HEAD_DIM = 128
REQ_GRP = 2
SCORE_LEN = 16

NEGATIVE = -1e30
EPSILON = 1e-05
LANES = 128
MESH = pl.DeviceIdType.MESH
F32 = jnp.float32
BF16 = jnp.bfloat16


def gather_events(sizes):
    events = [((0,) * len(sizes), -1)]
    for axis, size in enumerate(sizes):
        held = list(events)
        for offset, _ in held:
            for step in range(1, size):
                moved = list(offset)
                moved[axis] = (size - step) % size
                events.append((tuple(moved), axis))
    return events


def forward_blocks(sizes, here, place, to_device, send_sem, recv_sem):
    def owner_of(offset):
        return [lax.rem(here[a] + offset[a], sizes[a]) if offset[a] else here[a] for a in range(len(sizes))]

    def copy(owner, target, sem):
        ref, slot = place(owner)
        return pltpu.make_async_remote_copy(
            src_ref=ref,
            dst_ref=ref,
            send_sem=sem,
            recv_sem=recv_sem.at[slot],
            device_id=to_device(target),
            device_id_type=MESH,
        )

    state = {"sent": 0, "copies": []}

    def step(event):
        offset, via = event
        owner = owner_of(offset)
        if via >= 0:
            copy(owner, here_next, send_sem.at[0]).wait_recv()
        for axis in range(via + 1, len(sizes)):
            for move in range(1, sizes[axis]):
                target = list(here)
                target[axis] = lax.rem(here[axis] + move, sizes[axis])
                out = copy(owner, target, send_sem.at[state["sent"]])
                out.start()
                state["sent"] += 1
                state["copies"].append(out)

    here_next = list(here)
    here_next[-1] = lax.rem(here[-1] + 1, sizes[-1])
    return step, state["copies"]


def kernel(
    groups,
    shards,
    query_ref,
    own_key_ref,
    own_value_ref,
    key_hbm,
    value_hbm,
    key_owner_ref,
    key_place_ref,
    token_place_ref,
    target_ref,
    proj_hbm,
    residual_ref,
    gain_ref,
    bias_ref,
    vocab_hbm,
    out_ref,
    keys,
    values,
    proj,
    vocab,
    all_query,
    part_num,
    part_stat,
    got_num,
    got_stat,
    attended,
    mixed,
    got_mixed,
    normed,
    stats,
    got_stats,
    local_sem,
    query_send,
    query_recv,
    part_send,
    part_recv,
    mixed_send,
    mixed_recv,
    norm_send_a,
    norm_recv_a,
    norm_send_b,
    norm_recv_b,
    stat_send,
    stat_recv,
):
    group = lax.axis_index("group")
    shard = lax.axis_index("tensor")
    devices = groups * shards
    size_x = shards // 2
    size_y = size_x
    size_z = groups // size_y
    at_z, at_y = group // size_y, lax.rem(group, size_y)
    at_x, core = shard // 2, lax.rem(shard, 2)
    me = group * shards + shard
    tok_grp = query_ref.shape[1]
    flat_width = query_ref.shape[2]
    heads = flat_width // HEAD_DIM
    width = gain_ref.shape[1]
    half_width = width // 2
    rows = tok_grp // shards
    rows_two = 2 * rows
    score_scale = 1.0 / math.sqrt(HEAD_DIM)

    loads = [
        pltpu.make_async_copy(key_hbm, keys, local_sem.at[0]),
        pltpu.make_async_copy(value_hbm, values, local_sem.at[1]),
        pltpu.make_async_copy(proj_hbm, proj, local_sem.at[2]),
        pltpu.make_async_copy(vocab_hbm, vocab, local_sem.at[3]),
    ]
    for load in loads:
        load.start()

    barrier = pltpu.get_barrier_semaphore()

    def greet(step, carry):
        other = lax.rem(me + step, devices)
        pl.semaphore_signal(
            barrier, inc=1, device_id=(other // shards, lax.rem(other, shards)), device_id_type=MESH
        )
        return carry

    all_query[group] = query_ref[...]
    lax.fori_loop(1, devices, greet, 0)
    pl.semaphore_wait(barrier, devices - 1)

    def query_place(owner):
        slot = owner[0] * size_y + owner[1]
        return all_query.at[slot], slot

    sizes = (size_z, size_y)
    query_step, query_copies = forward_blocks(
        sizes,
        [at_z, at_y],
        query_place,
        lambda target: (target[0] * size_y + target[1], shard),
        query_send,
        query_recv,
    )
    for event in gather_events(sizes):
        query_step(event)

    def head_slope(head):
        exponent = (shard * heads + head + 1).astype(F32) * (-8.0 / HEADS)
        return jnp.exp2(jnp.full((1, 1), exponent, F32))

    own_row = lax.broadcasted_iota(jnp.int32, (tok_grp, tok_grp), 0)
    own_column = lax.broadcasted_iota(jnp.int32, (tok_grp, tok_grp), 1)
    own_allowed = (own_row // SCORE_LEN == own_column // SCORE_LEN) & (own_column <= own_row)
    own_distance = (own_row - own_column).astype(F32)
    own_parts = {}
    for model in range(2):
        for head in range(heads):
            span = slice(head * HEAD_DIM, (head + 1) * HEAD_DIM)
            scores = lax.dot_general(
                query_ref[model, :, span],
                own_key_ref[model, :, span],
                (((1,), (1,)), ((), ())),
                preferred_element_type=F32,
            )
            scores = scores * score_scale - head_slope(head) * own_distance
            scores = jnp.where(own_allowed, scores, NEGATIVE)
            top = jnp.max(scores, axis=1, keepdims=True)
            terms = jnp.where(own_allowed, jnp.exp(scores - top), 0.0)
            total = jnp.sum(terms, axis=1, keepdims=True)
            number = jnp.dot(
                terms.astype(BF16), own_value_ref[model, :, span], preferred_element_type=F32
            )
            own_parts[model, head] = (top, total, number)

    loads[0].wait()
    loads[1].wait()
    block = min(groups, 8)
    token_count = block * tok_grp
    key_count = keys.shape[1]

    def attend(index, carry):
        first = index * block
        token = lax.broadcasted_iota(jnp.int32, (token_count, 1), 0) + first * tok_grp
        token_owner = token // SCORE_LEN
        place = token_place_ref[pl.ds(pl.multiple_of(first * tok_grp, token_count), token_count), :]
        allowed = token_owner == key_owner_ref[...]
        distance = (place - key_place_ref[...]).astype(F32)
        lane = lax.broadcasted_iota(jnp.int32, (token_count, LANES), 1)
        packed = jnp.zeros((token_count, LANES), F32)
        for model in range(2):
            for head in range(heads):
                span = slice(head * HEAD_DIM, (head + 1) * HEAD_DIM)
                asked = all_query[pl.ds(first, block), model, :, span].reshape(token_count, HEAD_DIM)
                scores = lax.dot_general(
                    asked,
                    keys[model, :, span],
                    (((1,), (1,)), ((), ())),
                    preferred_element_type=F32,
                )
                scores = scores * score_scale - head_slope(head) * distance
                scores = jnp.where(allowed, scores, NEGATIVE)
                top = jnp.max(scores, axis=1, keepdims=True)
                terms = jnp.where(allowed, jnp.exp(scores - top), 0.0)
                total = jnp.sum(terms, axis=1, keepdims=True)
                number = jnp.dot(
                    terms.astype(BF16), values[model, :, span], preferred_element_type=F32
                )
                part_num[pl.ds(first, block), model, :, span] = number.astype(BF16).reshape(
                    block, tok_grp, HEAD_DIM
                )
                column = model * heads + head
                packed = jnp.where(lane == column, top, packed)
                packed = jnp.where(lane == column + 64, total, packed)
        part_stat[pl.ds(first, block)] = packed.reshape(block, tok_grp, LANES)
        return carry

    lax.fori_loop(0, groups // block, attend, 0)

    part_copies = []
    for step in range(1, groups):
        other = lax.rem(group + step, groups)
        for which, (source, landing) in enumerate(((part_num, got_num), (part_stat, got_stat))):
            copy = pltpu.make_async_remote_copy(
                src_ref=source.at[other],
                dst_ref=landing.at[group],
                send_sem=part_send.at[which, step],
                recv_sem=part_recv.at[which, step],
                device_id=(other, shard),
                device_id_type=MESH,
            )
            copy.start()
            part_copies.append(copy)
    for copy in part_copies:
        copy.wait_recv()

    sources = [(part_num, part_stat, group)]
    for step in range(1, groups):
        sources.append((got_num, got_stat, lax.rem(group + step, groups)))
    source_stats = [stat[index] for _, stat, index in sources]
    for model in range(2):
        for head in range(heads):
            span = slice(head * HEAD_DIM, (head + 1) * HEAD_DIM)
            column = model * heads + head
            own_top, own_total, own_number = own_parts[model, head]
            top = own_top
            for stat in source_stats:
                top = jnp.maximum(top, stat[:, column : column + 1])
            scale = jnp.exp(own_top - top)
            total = own_total * scale
            number = own_number * scale
            for stat, (num, _, index) in zip(source_stats, sources):
                scale = jnp.exp(stat[:, column : column + 1] - top)
                total = total + scale * stat[:, column + 64 : column + 65]
                number = number + scale * num[index, model, :, span].astype(F32)
            attended[model, :, span] = (number / total).astype(BF16)

    loads[2].wait()
    row_shard = lax.broadcasted_iota(jnp.int32, (tok_grp, 1), 0) // rows
    for model in range(2):
        product = jnp.dot(attended[model], proj[model], preferred_element_type=F32)
        held = jnp.concatenate([residual_ref[model].astype(F32)] * shards, axis=0)
        product = product + jnp.where(row_shard == shard, held, 0.0)
        for part in range(shards // 2):
            mixed[model, part] = product[part * rows_two : (part + 1) * rows_two]

    mixed_copies = []
    for step in range(1, shards):
        other = lax.rem(shard + step, shards)
        copy = pltpu.make_async_remote_copy(
            src_ref=mixed.at[lax.rem(other, 2), other // 2],
            dst_ref=got_mixed.at[shard],
            send_sem=mixed_send.at[step],
            recv_sem=mixed_recv.at[step],
            device_id=(group, other),
            device_id_type=MESH,
        )
        copy.start()
        mixed_copies.append(copy)
    hidden = mixed[core, at_x]
    for copy in mixed_copies:
        copy.wait_recv()
    for step in range(1, shards):
        hidden = hidden + got_mixed[lax.rem(shard + step, shards)]
    mean = jnp.mean(hidden, axis=1, keepdims=True)
    centered = hidden - mean
    variance = jnp.mean(centered * centered, axis=1, keepdims=True)
    gain = jnp.where(core == 0, gain_ref[0:1, :], gain_ref[1:2, :])
    bias = jnp.where(core == 0, bias_ref[0:1, :], bias_ref[1:2, :])
    result = (centered / jnp.sqrt(variance + EPSILON) * gain + bias).astype(BF16)
    my_slot = group * size_x + at_x
    normed[0, core, my_slot] = result[:, :half_width]
    normed[1, core, my_slot] = result[:, half_width:]

    slots = groups * size_x

    def norm_place_a(owner):
        slot = (owner[0] * size_y + owner[1]) * size_x + owner[2]
        return normed.at[0, owner[3], slot], owner[3] * slots + slot

    def norm_place_b(owner):
        slot = (owner[0] * size_y + owner[2]) * size_x + owner[1]
        return normed.at[1, owner[3], slot], owner[3] * slots + slot

    sizes_a = (size_z, size_y, size_x, 2)
    sizes_b = (size_z, size_x, size_y, 2)
    step_a, copies_a = forward_blocks(
        sizes_a,
        [at_z, at_y, at_x, core],
        norm_place_a,
        lambda to: (to[0] * size_y + to[1], to[2] * 2 + to[3]),
        norm_send_a,
        norm_recv_a,
    )
    step_b, copies_b = forward_blocks(
        sizes_b,
        [at_z, at_x, at_y, core],
        norm_place_b,
        lambda to: (to[0] * size_y + to[2], to[1] * 2 + to[3]),
        norm_send_b,
        norm_recv_b,
    )
    for event_a, event_b in zip(gather_events(sizes_a), gather_events(sizes_b)):
        step_a(event_a)
        step_b(event_b)

    loads[3].wait()
    words = vocab.shape[2]
    tokens = groups * tok_grp
    chunk = min(tokens, 256)
    chunk_slots = chunk // rows_two
    message = stats.shape[1]

    def score(index, carry):
        lane = lax.broadcasted_iota(jnp.int32, (chunk, LANES), 1)
        word = lax.broadcasted_iota(jnp.int32, (chunk, words), 1) + me * words
        packed = jnp.zeros((chunk, LANES), F32)
        wanted = target_ref[pl.ds(pl.multiple_of(index * chunk, chunk), chunk), :]
        for model in range(2):
            left = normed[0, model, pl.ds(index * chunk_slots, chunk_slots)].reshape(chunk, half_width)
            right = normed[1, model, pl.ds(index * chunk_slots, chunk_slots)].reshape(chunk, half_width)
            logits = jnp.dot(left, vocab[model, :half_width], preferred_element_type=F32)
            logits = logits + jnp.dot(right, vocab[model, half_width:], preferred_element_type=F32)
            peak = jnp.max(logits, axis=1, keepdims=True)
            total = jnp.sum(jnp.exp(logits - peak), axis=1, keepdims=True)
            chosen = jnp.sum(jnp.where(word == wanted, logits, 0.0), axis=1, keepdims=True)
            packed = jnp.where(lane == 3 * model, peak, packed)
            packed = jnp.where(lane == 3 * model + 1, total, packed)
            packed = jnp.where(lane == 3 * model + 2, chosen, packed)
        stats[pl.ds(index * (chunk // message), chunk // message)] = packed.reshape(
            chunk // message, message, LANES
        )
        return carry

    lax.fori_loop(0, tokens // chunk, score, 0)

    def stat_copy(step):
        other = lax.rem(me + step, devices)
        return pltpu.make_async_remote_copy(
            src_ref=stats.at[(other * rows) // message],
            dst_ref=got_stats.at[me],
            send_sem=stat_send.at[step],
            recv_sem=stat_recv.at[step],
            device_id=(other // shards, lax.rem(other, shards)),
            device_id_type=MESH,
        )

    def stat_start(step, carry):
        stat_copy(step).start()
        return carry

    def stat_finish(step, carry):
        stat_copy(step).wait()
        return carry

    lax.fori_loop(1, devices, stat_start, 0)
    got_stats[me] = stats[(me * rows) // message]
    for copy in query_copies + part_copies + mixed_copies + copies_a + copies_b:
        copy.wait_send()
    lax.fori_loop(1, devices, stat_finish, 0)

    gathered = got_stats[...]
    lane = lax.broadcasted_iota(jnp.int32, (message, LANES), 1)
    result = jnp.zeros((message, LANES), F32)
    for model in range(2):
        peaks = gathered[:, :, 3 * model : 3 * model + 1]
        peak = jnp.max(peaks, axis=0)
        total = jnp.sum(
            gathered[:, :, 3 * model + 1 : 3 * model + 2] * jnp.exp(peaks - peak[None]), axis=0
        )
        chosen = jnp.sum(gathered[:, :, 3 * model + 2 : 3 * model + 3], axis=0)
        result = jnp.where(lane == model, chosen - (peak + jnp.log(total)), result)
    out_ref[...] = result


def per_device(
    query,
    self_kv,
    kv_pages,
    page_dest,
    page_request,
    score_len,
    out_proj,
    residual,
    norm_gain,
    norm_bias,
    vocab,
    targets,
):
    groups = lax.axis_size("group")
    shards = lax.axis_size("tensor")
    group_id = lax.axis_index("group")
    tensor_id = lax.axis_index("tensor")
    devices = groups * shards
    tok_grp = query.shape[1]
    flat_width = query.shape[2]
    heads = flat_width // HEAD_DIM
    per_owner = kv_pages.shape[1]
    page_len = kv_pages.shape[2]
    width = out_proj.shape[2]
    words = vocab.shape[2]
    page_total = page_dest.shape[0]
    tokens = groups * tok_grp
    rows = tok_grp // shards
    message = max(8, rows)
    key_count = per_owner * page_len

    combined = page_dest[:, 0] * REQ_GRP + page_request
    page_ids = jnp.arange(page_total, dtype=jnp.int32)
    key_ids = jnp.arange(key_count, dtype=jnp.int32)
    my_combined = lax.dynamic_slice_in_dim(combined, group_id * per_owner, per_owner)
    key_owner = jnp.repeat(my_combined, page_len)
    key_page = group_id * per_owner + key_ids // page_len
    earlier = (combined[:, None] == key_owner[None, :]) & (page_ids[:, None] < key_page[None, :])
    key_place = jnp.sum(earlier.astype(jnp.int32), axis=0) * page_len + key_ids % page_len
    token_ids = jnp.arange(tokens, dtype=jnp.int32)
    seen = (combined[None, :] == (token_ids // SCORE_LEN)[:, None]).astype(jnp.int32)
    token_place = jnp.sum(seen, axis=1) * page_len + token_ids % SCORE_LEN

    keys = kv_pages[:, :, :, 0].reshape(2, key_count, flat_width)
    values = kv_pages[:, :, :, 1].reshape(2, key_count, flat_width)

    vmem = pl.BlockSpec(memory_space=pltpu.VMEM)
    hbm = pl.BlockSpec(memory_space=pl.ANY)
    dma = pltpu.SemaphoreType.DMA
    result = pl.pallas_call(
        functools.partial(kernel, groups, shards),
        out_shape=jax.ShapeDtypeStruct((message, LANES), F32),
        in_specs=[vmem, vmem, vmem, hbm, hbm, vmem, vmem, vmem, vmem, hbm, vmem, vmem, vmem, hbm],
        out_specs=vmem,
        scratch_shapes=[
            pltpu.VMEM((2, key_count, flat_width), BF16),
            pltpu.VMEM((2, key_count, flat_width), BF16),
            pltpu.VMEM(out_proj.shape, BF16),
            pltpu.VMEM(vocab.shape, BF16),
            pltpu.VMEM((groups, 2, tok_grp, flat_width), BF16),
            pltpu.VMEM((groups, 2, tok_grp, flat_width), BF16),
            pltpu.VMEM((groups, tok_grp, LANES), F32),
            pltpu.VMEM((groups, 2, tok_grp, flat_width), BF16),
            pltpu.VMEM((groups, tok_grp, LANES), F32),
            pltpu.VMEM((2, tok_grp, flat_width), BF16),
            pltpu.VMEM((2, shards // 2, 2 * rows, width), F32),
            pltpu.VMEM((shards, 2 * rows, width), F32),
            pltpu.VMEM((2, 2, devices // 2, 2 * rows, width // 2), BF16),
            pltpu.VMEM((tokens // message, message, LANES), F32),
            pltpu.VMEM((devices, message, LANES), F32),
            dma((4,)),
            dma((groups,)),
            dma((groups,)),
            dma((2, groups)),
            dma((2, groups)),
            dma((shards,)),
            dma((shards,)),
            dma((devices,)),
            dma((devices,)),
            dma((devices,)),
            dma((devices,)),
            dma((devices,)),
            dma((devices,)),
        ],
        compiler_params=pltpu.CompilerParams(
            collective_id=0, has_side_effects=True, vmem_limit_bytes=56 * 1024 * 1024
        ),
        name="rollout_logprob",
    )(
        query,
        self_kv[:, :, 0],
        self_kv[:, :, 1],
        keys,
        values,
        key_owner[None, :],
        key_place[None, :],
        token_place[:, None],
        targets[:, None],
        out_proj,
        residual,
        norm_gain,
        norm_bias,
        vocab,
    )
    first = lax.rem(tensor_id * rows, message)
    mine = jnp.transpose(lax.dynamic_slice(result, (first, 0), (rows, 2)))
    local_ids = tensor_id * rows + jnp.arange(rows, dtype=jnp.int32)
    keep_token = local_ids % SCORE_LEN < score_len[local_ids // SCORE_LEN]
    return jnp.where(keep_token[None, :], mine, 0.0)


def solution(mesh):
    in_specs = (
        P(None, "group", "tensor"),
        P(None, "group", None, "tensor"),
        P(None, "group", None, None, "tensor"),
        P(),
        P(),
        P("group"),
        P(None, "tensor", None),
        P(None, ("group", "tensor"), None),
        P(),
        P(),
        P(None, None, ("group", "tensor")),
        P(),
    )
    out_specs = P(None, ("group", "tensor"))
    return jax.shard_map(
        per_device, mesh=mesh, in_specs=in_specs, out_specs=out_specs, check_vma=False
    )
```

time: 426 us -> 89.6 us (0.21)
  waiting for transfers between devices: 203 us -> 0 us
  blocking collectives: 83 us -> 0 us
  local copies, waits for them, and re-layouts: 93.4 us -> 17.1 us
  Pallas kernels: 0 us -> 69.6 us
  matrix products: 14.1 us -> 0 us
  between operations: 13.8 us -> 0.11 us
  other arithmetic: 10.7 us -> 2.51 us
  starting transfers between devices: 7.67 us -> 0 us
    all_to_all x1 -> x0, waiting for transfers between devices: 126 us -> none  [per_device(): lax.all_to_all(outgoing, 'group', split_axis=1, concat_axis=1, tiled=True)]
    pallas_call x0 -> x1, Pallas kernels: none -> 69.6 us  [per_device(): pl.pallas_call(functools.partial(kernel, groups, shards), out_shape=jax.S...]
    all_gather x1 -> x0, waiting for transfers between devices: 55.8 us -> none  [per_device(): lax.all_gather(normed, ('group', 'tensor'), axis=1, tiled=True)]
    dot_general x1 -> x0, local copies, waits for them, and re-layouts: 47.6 us -> none  [per_device(): jnp.einsum('mnd,mdv->mnv', lax.all_gather(normed, ('group', 'tensor'), ax...]
    psum x1 -> x0, blocking collectives: 43.5 us -> none  [per_device(): lax.psum((jnp.sum(jnp.exp(logits - row_peak[..., None]), axis=2), jnp.whe...]
    pmax x1 -> x0, blocking collectives: 39.5 us -> none  [per_device(): row_peak = lax.pmax(jnp.max(logits, axis=2), ('group', 'tensor'))]
    reduce_scatter x1 -> x0, waiting for transfers between devices: 20.6 us -> none  [per_device(): lax.psum_scatter(jnp.einsum('mtk,mkd->tmd', attended, out_proj, preferred...]
    scatter x3 -> x0, local copies, waits for them, and re-layouts: 17.6 us -> none  [the longest x2 14.7 us: per_device(): outgoing = outgoing.at[:, my_dest * capacity + my_position].set(kv_pages)]
  transfers between devices with their start and end apart: 3 -> 0, of which waited for: 3 -> 0; matrix products, arithmetic and copies ran while one was open for 3% -> 0% of each run, Pallas kernels for 0% -> 0%
where the time goes in v1:
time: 89.6 us; the launch traced here: 89.3 us
  Pallas kernels  69.6 us (78%)
  local copies, waits for them, and re-layouts  17.1 us (19%)
  other arithmetic  2.51 us (3%)
    pallas_call x1, Pallas kernels, per_device(): pl.pallas_call(functools.partial(kernel, groups, shards), out_shape=jax.S...  69.6 us
    slice x1, local copies, waits for them, and re-layouts, per_device(): values = kv_pages[:, :, :, 1].reshape(2, key_count, flat_width)  8.7 us
    unnamed x10, local copies, waits for them, and re-layouts  3.39 us

profile of v1, /device:TPU:0, one launch (start us, length us, event | category | flops | bytes accessed | tf_op | source)
XLA Modules:
  0.0 89.3 jit_solution(3554394185235314315)
XLA Ops:
  0.0 0.0 copy-start
  0.0 1.2 %fusion.14 = (bf16[2,32,1,512]{3,2,1,0:T(2,128)(2,1)S(1)}, bf16[2,32,1,512]{3,2,1,0:T(2,128)(2,1)S(1)}) fusion(bf16[2,32,2,512]{3,2,1,0:T(2,128)(2,1)} %param.13), kind=kLoop, calls=%fused_computation.44 | loop fusion | bytes 262144 | tf_op jit(solution)/shard_map/slice | solution.py:515
  1.2 0.7 copy_bitcast_fusion
  1.9 8.7 %fusion.13 = (bf16[2,48,16,1,512]{4,3,2,1,0:T(2,128)(2,1)S(1)}, bf16[2,48,16,1,512]{4,3,2,1,0:T(2,128)(2,1)S(1)}) fusion(bf16[2,48,16,2,512]{4,3,2,1,0:T(2,128)(2,1)} %param.14), kind=kLoop, calls=%fused_computation.43 | loop fusion | bytes 6291456 | tf_op jit(solution)/shard_map/slice | solution.py:468
  10.6 1.7 %copy.32 = bf16[2,48,16,1,512]{4,2,1,0,3:T(8,128)(2,1)} copy(bf16[2,48,16,1,512]{4,3,2,1,0:T(2,128)(2,1)S(1)} %get-tuple-element.6) | data formatting | bytes 3145728
  12.3 0.0 copy-start.2
  12.3 0.0 copy-start.1
  12.3 0.0 copy-start.3
  12.3 1.7 %copy.33 = bf16[2,48,16,1,512]{4,2,1,0,3:T(8,128)(2,1)} copy(bf16[2,48,16,1,512]{4,3,2,1,0:T(2,128)(2,1)S(1)} %get-tuple-element.5) | data formatting | bytes 3145728
  14.0 0.0 copy-done.2
  14.0 0.0 copy-done.1
  14.0 0.1 dynamic_slice.7
  14.1 0.1 broadcast_in_dim.13
  14.2 0.7 broadcast_in_dim_reshape.4.key_owner_ref
  14.9 0.1 eq.35
  14.9 0.2 convert_reduce_fusion
  15.2 0.6 fusion.9.key_place_ref
  15.8 0.2 convert_reduce_fusion.1
  16.0 0.1 copy.27
  16.1 0.7 fusion.1.token_place_ref
  16.8 0.0 copy-done.3
  16.8 0.8 copy.28.target_ref
  17.6 69.6 %rollout_logprob.1 = f32[8,128]{1,0:T(8,128)} custom-call(bf16[2,32,512]{2,1,0:T(8,128)(2,1)} %query_ref.1, bf16[2,32,512]{2,1,0:T(8,128)(2,1)} %get-tuple-element.10.own_key_ref, bf16[2,32,512]{2,1,0:T(8,128)(2,1)} %get-tuple-element.9.own_value_ref, bf16[2,768,512]{2,1,0:T(8,128)(2,1)} %bitcast.12, bf16[2,768,512]{2,1,0:T(8,128)(2,1)} %bitcast.13, ...), custom_call_target="tpu_custom_call" | custom-call | tf_op jit(solution)/shard_map/rollout_logprob/pallas_call | solution.py:473
  87.3 0.0 copy-done
  87.3 0.6 gather_fusion
  87.9 0.8 select_bitcast_fusion
  88.7 0.6 copy.29
  (9 shorter events, 0.1 us)
Async XLA Ops:
  0.0 87.3 %copy-start = (s32[2]{0:T(128)S(1)}, s32[2]{0:T(128)}, u32[]{:S(2)}) copy-start(s32[2]{0:T(128)} %param.17) | copy-start | bytes 28
  12.3 1.7 %copy-start.2 = (s32[384,1]{0,1:T(1,128)S(1)}, s32[384,1]{0,1:T(1,128)}, u32[]{:S(2)}) copy-start(s32[384,1]{0,1:T(1,128)} %param.15) | copy-start | bytes 4612
  12.3 1.7 %copy-start.1 = (s32[384]{0:T(512)S(1)}, s32[384]{0:T(512)}, u32[]{:S(2)}) copy-start(s32[384]{0:T(512)} %param.16) | copy-start | bytes 4612
  12.3 4.5 %copy-start.3 = (s32[256]{0:T(256)S(1)}, s32[256]{0:T(256)}, u32[]{:S(2)}) copy-start(s32[256]{0:T(256)} %param.23) | copy-start | bytes 3076

commit v2 on v1

v2 whole, which is shorter than its diff:
```python
import functools
import math

import jax
import jax.numpy as jnp
from jax import lax
from jax.experimental import pallas as pl
from jax.experimental.pallas import tpu as pltpu
from jax.sharding import PartitionSpec as P

HEADS = 16
HEAD_DIM = 128
REQ_GRP = 2
SCORE_LEN = 16

NEGATIVE = -1e30
EPSILON = 1e-05
LANES = 128
MESH = pl.DeviceIdType.MESH
F32 = jnp.float32
BF16 = jnp.bfloat16


def gather_events(sizes):
    events = [((0,) * len(sizes), -1)]
    for axis, size in enumerate(sizes):
        held = list(events)
        for offset, _ in held:
            for step in range(1, size):
                moved = list(offset)
                moved[axis] = (size - step) % size
                events.append((tuple(moved), axis))
    return events


def forward_blocks(sizes, here, place, to_device, send_sem, recv_sem):
    def owner_of(offset):
        return [lax.rem(here[a] + offset[a], sizes[a]) if offset[a] else here[a] for a in range(len(sizes))]

    def copy(owner, target, sem):
        ref, slot = place(owner)
        return pltpu.make_async_remote_copy(
            src_ref=ref,
            dst_ref=ref,
            send_sem=sem,
            recv_sem=recv_sem.at[slot],
            device_id=to_device(target),
            device_id_type=MESH,
        )

    state = {"sent": 0, "copies": []}

    def step(event):
        offset, via = event
        owner = owner_of(offset)
        if via >= 0:
            copy(owner, here_next, send_sem.at[0]).wait_recv()
        for axis in range(via + 1, len(sizes)):
            for move in range(1, sizes[axis]):
                target = list(here)
                target[axis] = lax.rem(here[axis] + move, sizes[axis])
                out = copy(owner, target, send_sem.at[state["sent"]])
                out.start()
                state["sent"] += 1
                state["copies"].append(out)

    here_next = list(here)
    here_next[-1] = lax.rem(here[-1] + 1, sizes[-1])
    return step, state["copies"]


def split_pairs(pairs):
    count = pairs.shape[0]
    row = lax.broadcasted_iota(jnp.int32, (count, count), 0)
    column = lax.broadcasted_iota(jnp.int32, (count, count), 1)
    wanted = jnp.where(row < count // 2, 2 * row, 2 * row - count + 1)
    chooser = jnp.where(column == wanted, 1.0, 0.0).astype(BF16)
    return jnp.dot(chooser, pairs, preferred_element_type=F32).astype(BF16)


def to_column(row):
    count = row.shape[1]
    down = lax.broadcasted_iota(jnp.int32, (count, count), 0)
    across = lax.broadcasted_iota(jnp.int32, (count, count), 1)
    return jnp.sum(jnp.where(down == across, row, 0), axis=1, keepdims=True)


def kernel(
    groups,
    shards,
    page_len,
    query_ref,
    own_ref,
    pages_hbm,
    dest_ref,
    request_ref,
    score_len_ref,
    target_ref,
    proj_hbm,
    residual_ref,
    gain_ref,
    bias_ref,
    vocab_hbm,
    out_ref,
    pages,
    keys,
    values,
    proj,
    vocab,
    all_query,
    part_num,
    part_stat,
    got_num,
    got_stat,
    attended,
    mixed,
    got_core,
    got_mixed,
    normed,
    stats,
    got_stats,
    local_sem,
    query_send,
    query_recv,
    part_send,
    part_recv,
    core_send,
    core_recv,
    mixed_send,
    mixed_recv,
    norm_send_a,
    norm_recv_a,
    norm_send_b,
    norm_recv_b,
    stat_send,
    stat_recv,
):
    group = lax.axis_index("group")
    shard = lax.axis_index("tensor")
    devices = groups * shards
    size_x = shards // 2
    size_y = size_x
    size_z = groups // size_y
    at_z, at_y = group // size_y, lax.rem(group, size_y)
    at_x, core = shard // 2, lax.rem(shard, 2)
    me = group * shards + shard
    tok_grp = query_ref.shape[1]
    flat_width = query_ref.shape[2]
    heads = flat_width // HEAD_DIM
    width = gain_ref.shape[1]
    half_width = width // 2
    rows = tok_grp // shards
    rows_two = 2 * rows
    score_scale = 1.0 / math.sqrt(HEAD_DIM)
    key_count = keys.shape[1]

    loads = [
        pltpu.make_async_copy(pages_hbm, pages, local_sem.at[0]),
        pltpu.make_async_copy(proj_hbm, proj, local_sem.at[1]),
        pltpu.make_async_copy(vocab_hbm, vocab, local_sem.at[2]),
    ]
    for load in loads:
        load.start()

    barrier = pltpu.get_barrier_semaphore()

    def greet(step, carry):
        other = lax.rem(me + step, devices)
        pl.semaphore_signal(
            barrier, inc=1, device_id=(other // shards, lax.rem(other, shards)), device_id_type=MESH
        )
        return carry

    def query_slot(z, y):
        return y * size_z + z

    my_query = query_slot(at_z, at_y)
    all_query[my_query] = query_ref[...]
    lax.fori_loop(1, devices, greet, 0)

    page_owner = dest_ref[...] * REQ_GRP + to_column(request_ref[...])
    page_total = page_owner.shape[0]
    page_id = lax.broadcasted_iota(jnp.int32, (page_total, key_count), 0)
    key_id = lax.broadcasted_iota(jnp.int32, (1, key_count), 1)
    key_page = group * (key_count // page_len) + key_id // page_len
    key_owner = jnp.sum(jnp.where(page_id == key_page, page_owner, 0), axis=0, keepdims=True)
    earlier = (page_owner == key_owner) & (page_id < key_page)
    key_rank = jnp.sum(jnp.where(earlier, 1, 0), axis=0, keepdims=True)
    key_place = key_rank * page_len + lax.rem(key_id, page_len)
    request_lanes = -(-groups * REQ_GRP // LANES) * LANES
    request_id = lax.broadcasted_iota(jnp.int32, (page_total, request_lanes), 1)
    request_pages = jnp.sum(
        jnp.where(page_owner == request_id, 1, 0), axis=0, keepdims=True
    )
    wanted_words = to_column(target_ref[...])

    pl.semaphore_wait(barrier, devices - 1)

    def query_place(owner):
        slot = query_slot(owner[0], owner[1])
        return all_query.at[slot], slot

    sizes = (size_z, size_y)
    query_step, query_copies = forward_blocks(
        sizes,
        [at_z, at_y],
        query_place,
        lambda target: (target[0] * size_y + target[1], shard),
        query_send,
        query_recv,
    )
    query_events = gather_events(sizes)
    query_step(query_events[0])

    loads[0].wait()
    for model in range(2):
        for start in range(0, key_count, 128):
            block = split_pairs(pages[model, 2 * start : 2 * start + 256])
            keys[model, start : start + 128] = block[:128]
            values[model, start : start + 128] = block[128:]
    for event in query_events[1:]:
        if event[1] == 0:
            query_step(event)

    def head_slope(head):
        exponent = (shard * heads + head + 1).astype(F32) * (-8.0 / HEADS)
        return jnp.exp2(jnp.full((1, 1), exponent, F32))

    def attend_own():
        own_row = lax.broadcasted_iota(jnp.int32, (tok_grp, tok_grp), 0)
        own_column = lax.broadcasted_iota(jnp.int32, (tok_grp, tok_grp), 1)
        own_allowed = (own_row // SCORE_LEN == own_column // SCORE_LEN) & (own_column <= own_row)
        own_distance = (own_row - own_column).astype(F32)
        own_parts = {}
        for model in range(2):
            own_split = split_pairs(own_ref[model])
            for head in range(heads):
                span = slice(head * HEAD_DIM, (head + 1) * HEAD_DIM)
                scores = lax.dot_general(
                    query_ref[model, :, span],
                    own_split[:tok_grp, span],
                    (((1,), (1,)), ((), ())),
                    preferred_element_type=F32,
                )
                scores = scores * score_scale - head_slope(head) * own_distance
                scores = jnp.where(own_allowed, scores, NEGATIVE)
                top = jnp.max(scores, axis=1, keepdims=True)
                terms = jnp.where(own_allowed, jnp.exp(scores - top), 0.0)
                total = jnp.sum(terms, axis=1, keepdims=True)
                number = jnp.dot(
                    terms.astype(BF16), own_split[tok_grp:, span], preferred_element_type=F32
                )
                own_parts[model, head] = (top, total, number)
        return own_parts

    token_count = size_z * tok_grp

    def attend(y):
        first = y * size_z
        row = lax.broadcasted_iota(jnp.int32, (token_count, 1), 0)
        token_group = (row // tok_grp) * size_y + y
        token_owner = token_group * REQ_GRP + lax.rem(row, tok_grp) // SCORE_LEN
        lane = lax.broadcasted_iota(jnp.int32, (token_count, request_lanes), 1)
        context = jnp.sum(
            jnp.where(lane == token_owner, request_pages, 0), axis=1, keepdims=True
        )
        place = context * page_len + lax.rem(row, SCORE_LEN)
        allowed = token_owner == key_owner
        distance = (place - key_place).astype(F32)
        lane = lax.broadcasted_iota(jnp.int32, (token_count, LANES), 1)
        packed = jnp.zeros((token_count, LANES), F32)
        for model in range(2):
            for head in range(heads):
                span = slice(head * HEAD_DIM, (head + 1) * HEAD_DIM)
                asked = all_query[pl.ds(first, size_z), model, :, span]
                scores = lax.dot_general(
                    asked.reshape(token_count, HEAD_DIM),
                    keys[model, :, span],
                    (((1,), (1,)), ((), ())),
                    preferred_element_type=F32,
                )
                scores = scores * score_scale - head_slope(head) * distance
                scores = jnp.where(allowed, scores, NEGATIVE)
                top = jnp.max(scores, axis=1, keepdims=True)
                terms = jnp.where(allowed, jnp.exp(scores - top), 0.0)
                total = jnp.sum(terms, axis=1, keepdims=True)
                number = jnp.dot(
                    terms.astype(BF16), values[model, :, span], preferred_element_type=F32
                )
                part_num[pl.ds(first, size_z), model, :, span] = number.astype(BF16).reshape(
                    size_z, tok_grp, HEAD_DIM
                )
                column = model * heads + head
                packed = jnp.where(lane == column, top, packed)
                packed = jnp.where(lane == column + 64, total, packed)
        part_stat[pl.ds(first, size_z)] = packed.reshape(size_z, tok_grp, LANES)

    part_copies = []
    for step_y in range(size_y):
        for event in query_events[1:]:
            if event[1] == 1 and event[0][1] == step_y:
                query_step(event)
        y = lax.rem(at_y + step_y, size_y)
        attend(y)
        for step_z in range(size_z):
            if step_y == 0 and step_z == 0:
                continue
            z = lax.rem(at_z + step_z, size_z)
            for which, (source, landing) in enumerate(
                ((part_num, got_num), (part_stat, got_stat))
            ):
                copy = pltpu.make_async_remote_copy(
                    src_ref=source.at[query_slot(z, y)],
                    dst_ref=landing.at[my_query],
                    send_sem=part_send.at[which, step_y * size_z + step_z],
                    recv_sem=part_recv.at[which, step_y * size_z + step_z],
                    device_id=(z * size_y + y, shard),
                    device_id_type=MESH,
                )
                copy.start()
                part_copies.append(copy)
    own_parts = attend_own()
    for copy in part_copies:
        copy.wait_recv()

    sources = [(part_num, part_stat, my_query)]
    for step in range(1, groups):
        sources.append((got_num, got_stat, lax.rem(my_query + step, groups)))
    source_stats = [stat[index] for _, stat, index in sources]
    for model in range(2):
        for head in range(heads):
            span = slice(head * HEAD_DIM, (head + 1) * HEAD_DIM)
            column = model * heads + head
            own_top, own_total, own_number = own_parts[model, head]
            top = own_top
            for stat in source_stats:
                top = jnp.maximum(top, stat[:, column : column + 1])
            scale = jnp.exp(own_top - top)
            total = own_total * scale
            number = own_number * scale
            for stat, (num, _, index) in zip(source_stats, sources):
                scale = jnp.exp(stat[:, column : column + 1] - top)
                total = total + scale * stat[:, column + 64 : column + 65]
                number = number + scale * num[index, model, :, span].astype(F32)
            attended[model, :, span] = (number / total).astype(BF16)

    loads[1].wait()
    row_shard = lax.broadcasted_iota(jnp.int32, (tok_grp, 1), 0) // rows

    def project(model):
        product = jnp.dot(attended[model], proj[model], preferred_element_type=F32)
        held = jnp.concatenate([residual_ref[model].astype(F32)] * shards, axis=0)
        product = product + jnp.where(row_shard == shard, held, 0.0)
        for part in range(size_x):
            mixed[model, part] = product[part * rows_two : (part + 1) * rows_two]

    core_copies = []
    project(1 - core)
    for step in list(range(1, size_x)) + [0]:
        part = lax.rem(at_x + step, size_x)
        copy = pltpu.make_async_remote_copy(
            src_ref=mixed.at[1 - core, part],
            dst_ref=got_core.at[part],
            send_sem=core_send.at[step],
            recv_sem=core_recv.at[step],
            device_id=(group, at_x * 2 + 1 - core),
            device_id_type=MESH,
        )
        copy.start()
        core_copies.append(copy)
    project(core)
    mixed_copies = []
    for step in range(1, size_x):
        part = lax.rem(at_x + step, size_x)
        core_copies[step - 1].wait_recv()
        mixed[core, part] = mixed[core, part] + got_core[part]
        copy = pltpu.make_async_remote_copy(
            src_ref=mixed.at[core, part],
            dst_ref=got_mixed.at[at_x],
            send_sem=mixed_send.at[step],
            recv_sem=mixed_recv.at[step],
            device_id=(group, part * 2 + core),
            device_id_type=MESH,
        )
        copy.start()
        mixed_copies.append(copy)
    core_copies[-1].wait_recv()
    hidden = mixed[core, at_x] + got_core[at_x]
    for copy in mixed_copies:
        copy.wait_recv()
    for step in range(1, size_x):
        hidden = hidden + got_mixed[lax.rem(at_x + step, size_x)]
    mean = jnp.mean(hidden, axis=1, keepdims=True)
    centered = hidden - mean
    variance = jnp.mean(centered * centered, axis=1, keepdims=True)
    gain = jnp.where(core == 0, gain_ref[0:1, :], gain_ref[1:2, :])
    bias = jnp.where(core == 0, bias_ref[0:1, :], bias_ref[1:2, :])
    result = (centered / jnp.sqrt(variance + EPSILON) * gain + bias).astype(BF16)
    my_slot = group * size_x + at_x
    normed[0, core, my_slot] = result[:, :half_width]
    normed[1, core, my_slot] = result[:, half_width:]

    slots = groups * size_x

    def norm_place_a(owner):
        slot = (owner[0] * size_y + owner[1]) * size_x + owner[2]
        return normed.at[0, owner[3], slot], owner[3] * slots + slot

    def norm_place_b(owner):
        slot = (owner[0] * size_y + owner[2]) * size_x + owner[1]
        return normed.at[1, owner[3], slot], owner[3] * slots + slot

    sizes_a = (size_z, size_y, size_x, 2)
    sizes_b = (size_z, size_x, size_y, 2)
    step_a, copies_a = forward_blocks(
        sizes_a,
        [at_z, at_y, at_x, core],
        norm_place_a,
        lambda to: (to[0] * size_y + to[1], to[2] * 2 + to[3]),
        norm_send_a,
        norm_recv_a,
    )
    step_b, copies_b = forward_blocks(
        sizes_b,
        [at_z, at_x, at_y, core],
        norm_place_b,
        lambda to: (to[0] * size_y + to[2], to[1] * 2 + to[3]),
        norm_send_b,
        norm_recv_b,
    )
    paired = list(zip(gather_events(sizes_a), gather_events(sizes_b)))
    for event_a, event_b in paired:
        if event_a[1] < 3:
            step_a(event_a)
            step_b(event_b)

    loads[2].wait()
    words = vocab.shape[2]
    tokens = groups * tok_grp
    chunk = min(tokens, 256)
    chunk_slots = chunk // rows_two
    message = stats.shape[1]
    chunk_messages = chunk // message
    for turn in range(2):
        model = core if turn == 0 else 1 - core
        if turn == 1:
            for event_a, event_b in paired:
                if event_a[1] == 3:
                    step_a(event_a)
                    step_b(event_b)
        for index in range(tokens // chunk):
            lane = lax.broadcasted_iota(jnp.int32, (chunk, LANES), 1)
            word = lax.broadcasted_iota(jnp.int32, (chunk, words), 1) + me * words
            wanted = wanted_words[index * chunk : (index + 1) * chunk]
            span = slice(index * chunk_slots, (index + 1) * chunk_slots)
            left = normed[0, model, span].reshape(chunk, half_width)
            right = normed[1, model, span].reshape(chunk, half_width)
            logits = jnp.dot(left, vocab[model, :half_width], preferred_element_type=F32)
            logits = logits + jnp.dot(right, vocab[model, half_width:], preferred_element_type=F32)
            peak = jnp.max(logits, axis=1, keepdims=True)
            total = jnp.sum(jnp.exp(logits - peak), axis=1, keepdims=True)
            chosen = jnp.sum(jnp.where(word == wanted, logits, 0.0), axis=1, keepdims=True)
            place = slice(index * chunk_messages, (index + 1) * chunk_messages)
            if turn == 0:
                packed = jnp.zeros((chunk, LANES), F32)
            else:
                packed = stats[place].reshape(chunk, LANES)
            packed = jnp.where(lane == 3 * model, peak, packed)
            packed = jnp.where(lane == 3 * model + 1, total, packed)
            packed = jnp.where(lane == 3 * model + 2, chosen, packed)
            stats[place] = packed.reshape(chunk_messages, message, LANES)

    def stat_copy(step):
        other = lax.rem(me + step, devices)
        return pltpu.make_async_remote_copy(
            src_ref=stats.at[(other * rows) // message],
            dst_ref=got_stats.at[me],
            send_sem=stat_send.at[step],
            recv_sem=stat_recv.at[step],
            device_id=(other // shards, lax.rem(other, shards)),
            device_id_type=MESH,
        )

    def stat_start(step, carry):
        stat_copy(step).start()
        return carry

    def stat_finish(step, carry):
        stat_copy(step).wait()
        return carry

    lax.fori_loop(1, devices, stat_start, 0)
    got_stats[me] = stats[(me * rows) // message]
    for copy in query_copies + part_copies + core_copies + mixed_copies + copies_a + copies_b:
        copy.wait_send()
    lax.fori_loop(1, devices, stat_finish, 0)

    gathered = got_stats[...]
    down = lax.broadcasted_iota(jnp.int32, (message, LANES), 0)
    across = lax.broadcasted_iota(jnp.int32, (message, LANES), 1)
    turned = down == across + lax.rem(shard * rows, message)
    local = shard * rows + lax.broadcasted_iota(jnp.int32, (1, LANES), 1)
    limit = jnp.where(local // SCORE_LEN == 0, score_len_ref[0], score_len_ref[1])
    keep = lax.rem(local, SCORE_LEN) < limit
    for model in range(2):
        peaks = gathered[:, :, 3 * model : 3 * model + 1]
        peak = jnp.max(peaks, axis=0)
        total = jnp.sum(
            gathered[:, :, 3 * model + 1 : 3 * model + 2] * jnp.exp(peaks - peak[None]), axis=0
        )
        chosen = jnp.sum(gathered[:, :, 3 * model + 2 : 3 * model + 3], axis=0)
        column = chosen - (peak + jnp.log(total))
        row = jnp.sum(jnp.where(turned, column, 0.0), axis=0, keepdims=True)
        out_ref[model : model + 1, :] = jnp.where(keep, row, 0.0)[:, :rows]


def per_device(
    query,
    self_kv,
    kv_pages,
    page_dest,
    page_request,
    score_len,
    out_proj,
    residual,
    norm_gain,
    norm_bias,
    vocab,
    targets,
):
    groups = lax.axis_size("group")
    shards = lax.axis_size("tensor")
    devices = groups * shards
    tok_grp = query.shape[1]
    flat_width = query.shape[2]
    page_len = kv_pages.shape[2]
    width = out_proj.shape[2]
    tokens = groups * tok_grp
    rows = tok_grp // shards
    message = max(8, rows)
    key_count = kv_pages.shape[1] * page_len
    size_x = shards // 2

    vmem = pl.BlockSpec(memory_space=pltpu.VMEM)
    smem = pl.BlockSpec(memory_space=pltpu.SMEM)
    hbm = pl.BlockSpec(memory_space=pl.ANY)
    dma = pltpu.SemaphoreType.DMA
    return pl.pallas_call(
        functools.partial(kernel, groups, shards, page_len),
        out_shape=jax.ShapeDtypeStruct((2, rows), F32),
        in_specs=[vmem, vmem, hbm, vmem, vmem, smem, vmem, hbm, vmem, vmem, vmem, hbm],
        out_specs=vmem,
        scratch_shapes=[
            pltpu.VMEM((2, 2 * key_count, flat_width), BF16),
            pltpu.VMEM((2, key_count, flat_width), BF16),
            pltpu.VMEM((2, key_count, flat_width), BF16),
            pltpu.VMEM(out_proj.shape, BF16),
            pltpu.VMEM(vocab.shape, BF16),
            pltpu.VMEM((groups, 2, tok_grp, flat_width), BF16),
            pltpu.VMEM((groups, 2, tok_grp, flat_width), BF16),
            pltpu.VMEM((groups, tok_grp, LANES), F32),
            pltpu.VMEM((groups, 2, tok_grp, flat_width), BF16),
            pltpu.VMEM((groups, tok_grp, LANES), F32),
            pltpu.VMEM((2, tok_grp, flat_width), BF16),
            pltpu.VMEM((2, size_x, 2 * rows, width), F32),
            pltpu.VMEM((size_x, 2 * rows, width), F32),
            pltpu.VMEM((size_x, 2 * rows, width), F32),
            pltpu.VMEM((2, 2, devices // 2, 2 * rows, width // 2), BF16),
            pltpu.VMEM((tokens // message, message, LANES), F32),
            pltpu.VMEM((devices, message, LANES), F32),
            dma((3,)),
            dma((groups,)),
            dma((groups,)),
            dma((2, groups)),
            dma((2, groups)),
            dma((size_x,)),
            dma((size_x,)),
            dma((size_x,)),
            dma((size_x,)),
            dma((devices,)),
            dma((devices,)),
            dma((devices,)),
            dma((devices,)),
            dma((devices,)),
            dma((devices,)),
        ],
        compiler_params=pltpu.CompilerParams(
            collective_id=0, has_side_effects=True, vmem_limit_bytes=56 * 1024 * 1024
        ),
        name="rollout_logprob",
    )(
        query,
        self_kv.reshape(2, 2 * tok_grp, flat_width),
        kv_pages.reshape(2, 2 * key_count, flat_width),
        page_dest,
        page_request[None, :],
        score_len,
        targets[None, :],
        out_proj,
        residual,
        norm_gain,
        norm_bias,
        vocab,
    )


def solution(mesh):
    in_specs = (
        P(None, "group", "tensor"),
        P(None, "group", None, "tensor"),
        P(None, "group", None, None, "tensor"),
        P(),
        P(),
        P("group"),
        P(None, "tensor", None),
        P(None, ("group", "tensor"), None),
        P(),
        P(),
        P(None, None, ("group", "tensor")),
        P(),
    )
    out_specs = P(None, ("group", "tensor"))
    return jax.shard_map(
        per_device, mesh=mesh, in_specs=in_specs, out_specs=out_specs, check_vma=False
    )
```

time: 89.6 us -> 77.8 us (0.87)
  local copies, waits for them, and re-layouts: 17.1 us -> 11.3 us
  Pallas kernels: 69.6 us -> 66.1 us
  other arithmetic: 2.51 us -> 0 us
    slice x2 -> x0, local copies, waits for them, and re-layouts: 9.9 us -> none  [the longest x1 8.7 us: per_device(): values = kv_pages[:, :, :, 1].reshape(2, key_count, flat_width)]
    reshape x0 -> x2, local copies, waits for them, and re-layouts: none -> 7.34 us  [the longest x1 5.74 us: per_device(): kv_pages.reshape(2, 2 * key_count, flat_width)]
    pallas_call x1, Pallas kernels: 69.6 us -> 66.1 us  [per_device(): pl.pallas_call(functools.partial(kernel, groups, shards, page_len), out_s...]
    add x4 -> x0, other arithmetic: 1.27 us -> none  [the longest x1 0.67 us: per_device(): token_place = jnp.sum(seen, axis=1) * page_len + token_ids % SCORE_LEN]
    unnamed x10 -> x2, local copies, waits for them, and re-layouts: 3.39 us -> 2.74 us
where the time goes in v2:
time: 77.8 us; the launch traced here: 77.5 us
  Pallas kernels  66.1 us (85%)
  local copies, waits for them, and re-layouts  11.3 us (15%)
    pallas_call x1, Pallas kernels, per_device(): pl.pallas_call(functools.partial(kernel, groups, shards, page_len), out_s...  66.1 us
    reshape x1, local copies, waits for them, and re-layouts, per_device(): kv_pages.reshape(2, 2 * key_count, flat_width)  5.74 us
    unnamed x2, local copies, waits for them, and re-layouts  2.74 us
    reshape x1, local copies, waits for them, and re-layouts, per_device(): self_kv.reshape(2, 2 * tok_grp, flat_width)  1.6 us

profile of v2, /device:TPU:0, one launch (start us, length us, event | category | flops | bytes accessed | tf_op | source)
XLA Modules:
  0.0 77.5 jit_solution(15271648419316917525)
XLA Ops:
  0.0 1.3 %broadcast_in_dim.6.request_ref = s32[1,384]{1,0:T(1,128)} reshape(s32[384]{0:T(512)} %param.16) | data formatting | bytes 3072 | tf_op jit(solution)/shard_map/broadcast_in_dim | solution.py:596
  1.3 1.6 %reshape.6.own_ref = bf16[2,64,512]{2,1,0:T(8,128)(2,1)} reshape(bf16[2,32,2,512]{3,2,1,0:T(2,128)(2,1)} %param.13) | data formatting | bytes 262144 | tf_op jit(solution)/shard_map/reshape | solution.py:593
  2.9 1.5 %copy.13.dest_ref = s32[384,1]{1,0:T(8,128)} copy(s32[384,1]{0,1:T(1,128)} %param.15) | data formatting | bytes 3072 | tf_op args[3]
  4.4 5.7 %reshape.7.pages_hbm = bf16[2,1536,512]{2,1,0:T(8,128)(2,1)} reshape(bf16[2,48,16,2,512]{4,3,2,1,0:T(2,128)(2,1)} %param.14) | data formatting | bytes 6291456 | tf_op jit(solution)/shard_map/reshape | solution.py:594
  10.1 66.1 %rollout_logprob.1 = f32[2,8]{1,0:T(2,128)} custom-call(bf16[2,32,512]{2,1,0:T(8,128)(2,1)} %query_ref.1, bf16[2,64,512]{2,1,0:T(8,128)(2,1)} %reshape.6.own_ref, bf16[2,1536,512]{2,1,0:T(8,128)(2,1)} %reshape.7.pages_hbm, s32[384,1]{1,0:T(8,128)} %copy.13.dest_ref, s32[1,384]{1,0:T(1,128)} %broadcast_in_dim.6.request_ref, s32[2]{0:T(128)} %score_len_ref.1, ...), custom_call_target="tpu_custom_call" | custom-call | tf_op jit(solution)/shard_map/rollout_logprob/pallas_call | solution.py:548
  76.2 1.2 %copy.15 = f32[2,8]{1,0:T(2,128)} copy(f32[2,8]{1,0:T(2,128)} %rollout_logprob.1) | data formatting | bytes 128

commit v3 on v2

--- a/solution.py
+++ b/solution.py
@@ -15,6 +15,8 @@
 
 NEGATIVE = -1e30
 EPSILON = 1e-05
+UNSEEN = 1e30
+LOWEST_TOP = -1e26
 LANES = 128
 MESH = pl.DeviceIdType.MESH
 F32 = jnp.float32
@@ -67,15 +69,6 @@
     here_next = list(here)
     here_next[-1] = lax.rem(here[-1] + 1, sizes[-1])
     return step, state["copies"]
-
-
-def split_pairs(pairs):
-    count = pairs.shape[0]
-    row = lax.broadcasted_iota(jnp.int32, (count, count), 0)
-    column = lax.broadcasted_iota(jnp.int32, (count, count), 1)
-    wanted = jnp.where(row < count // 2, 2 * row, 2 * row - count + 1)
-    chooser = jnp.where(column == wanted, 1.0, 0.0).astype(BF16)
-    return jnp.dot(chooser, pairs, preferred_element_type=F32).astype(BF16)
 
 
 def to_column(row):
@@ -102,7 +95,6 @@
     bias_ref,
     vocab_hbm,
     out_ref,
-    pages,
     keys,
     values,
     proj,
@@ -152,10 +144,11 @@
     rows = tok_grp // shards
     rows_two = 2 * rows
     score_scale = 1.0 / math.sqrt(HEAD_DIM)
-    key_count = keys.shape[1]
+    key_count = keys.shape[1] * page_len
 
     loads = [
-        pltpu.make_async_copy(pages_hbm, pages, local_sem.at[0]),
+        pltpu.make_async_copy(pages_hbm.at[:, :, 0], keys, local_sem.at[0]),
+        pltpu.make_async_copy(pages_hbm.at[:, :, 1], values, local_sem.at[3]),
         pltpu.make_async_copy(proj_hbm, proj, local_sem.at[1]),
         pltpu.make_async_copy(vocab_hbm, vocab, local_sem.at[2]),
     ]
@@ -167,7 +160,7 @@
     def greet(step, carry):
         other = lax.rem(me + step, devices)
         pl.semaphore_signal(
-            barrier, inc=1, device_id=(other // shards, lax.rem(other, shards)), device_id_type=MESH
+            barrier, inc=1, device_id=(lax.div(other, shards), lax.rem(other, shards)), device_id_type=MESH
         )
         return carry
 
@@ -178,7 +171,10 @@
     all_query[my_query] = query_ref[...]
     lax.fori_loop(1, devices, greet, 0)
 
-    page_owner = dest_ref[...] * REQ_GRP + to_column(request_ref[...])
+    requests = jnp.concatenate(
+        [request_ref[line : line + 1, :] for line in range(request_ref.shape[0])], axis=1
+    )
+    page_owner = to_column(dest_ref[...] * REQ_GRP + requests)
     page_total = page_owner.shape[0]
     page_id = lax.broadcasted_iota(jnp.int32, (page_total, key_count), 0)
     key_id = lax.broadcasted_iota(jnp.int32, (1, key_count), 1)
@@ -212,12 +208,6 @@
     query_events = gather_events(sizes)
     query_step(query_events[0])
 
-    loads[0].wait()
-    for model in range(2):
-        for start in range(0, key_count, 128):
-            block = split_pairs(pages[model, 2 * start : 2 * start + 256])
-            keys[model, start : start + 128] = block[:128]
-            values[model, start : start + 128] = block[128:]
     for event in query_events[1:]:
         if event[1] == 0:
             query_step(event)
@@ -233,12 +223,13 @@
         own_distance = (own_row - own_column).astype(F32)
         own_parts = {}
         for model in range(2):
-            own_split = split_pairs(own_ref[model])
+            own_keys = own_ref[model, :, 0, :]
+            own_values = own_ref[model, :, 1, :]
             for head in range(heads):
                 span = slice(head * HEAD_DIM, (head + 1) * HEAD_DIM)
                 scores = lax.dot_general(
                     query_ref[model, :, span],
-                    own_split[:tok_grp, span],
+                    own_keys[:, span],
                     (((1,), (1,)), ((), ())),
                     preferred_element_type=F32,
                 )
@@ -248,7 +239,7 @@
                 terms = jnp.where(own_allowed, jnp.exp(scores - top), 0.0)
                 total = jnp.sum(terms, axis=1, keepdims=True)
                 number = jnp.dot(
-                    terms.astype(BF16), own_split[tok_grp:, span], preferred_element_type=F32
+                    terms.astype(BF16), own_values[:, span], preferred_element_type=F32
                 )
                 own_parts[model, head] = (top, total, number)
         return own_parts
@@ -266,7 +257,7 @@
         )
         place = context * page_len + lax.rem(row, SCORE_LEN)
         allowed = token_owner == key_owner
-        distance = (place - key_place).astype(F32)
+        distance = jnp.where(allowed, (place - key_place).astype(F32), UNSEEN)
         lane = lax.broadcasted_iota(jnp.int32, (token_count, LANES), 1)
         packed = jnp.zeros((token_count, LANES), F32)
         for model in range(2):
@@ -275,17 +266,18 @@
                 asked = all_query[pl.ds(first, size_z), model, :, span]
                 scores = lax.dot_general(
                     asked.reshape(token_count, HEAD_DIM),
-                    keys[model, :, span],
+                    keys[model, :, :, span].reshape(key_count, HEAD_DIM),
                     (((1,), (1,)), ((), ())),
                     preferred_element_type=F32,
                 )
                 scores = scores * score_scale - head_slope(head) * distance
-                scores = jnp.where(allowed, scores, NEGATIVE)
-                top = jnp.max(scores, axis=1, keepdims=True)
-                terms = jnp.where(allowed, jnp.exp(scores - top), 0.0)
+                top = jnp.maximum(jnp.max(scores, axis=1, keepdims=True), LOWEST_TOP)
+                terms = jnp.exp(scores - top)
                 total = jnp.sum(terms, axis=1, keepdims=True)
                 number = jnp.dot(
-                    terms.astype(BF16), values[model, :, span], preferred_element_type=F32
+                    terms.astype(BF16),
+                    values[model, :, :, span].reshape(key_count, HEAD_DIM),
+                    preferred_element_type=F32,
                 )
                 part_num[pl.ds(first, size_z), model, :, span] = number.astype(BF16).reshape(
                     size_z, tok_grp, HEAD_DIM
@@ -294,6 +286,9 @@
                 packed = jnp.where(lane == column, top, packed)
                 packed = jnp.where(lane == column + 64, total, packed)
         part_stat[pl.ds(first, size_z)] = packed.reshape(size_z, tok_grp, LANES)
+
+    loads[0].wait()
+    loads[1].wait()
 
     part_copies = []
     for step_y in range(size_y):
@@ -344,7 +339,7 @@
                 number = number + scale * num[index, model, :, span].astype(F32)
             attended[model, :, span] = (number / total).astype(BF16)
 
-    loads[1].wait()
+    loads[2].wait()
     row_shard = lax.broadcasted_iota(jnp.int32, (tok_grp, 1), 0) // rows
 
     def project(model):
@@ -434,7 +429,7 @@
             step_a(event_a)
             step_b(event_b)
 
-    loads[2].wait()
+    loads[3].wait()
     words = vocab.shape[2]
     tokens = groups * tok_grp
     chunk = min(tokens, 256)
@@ -473,11 +468,11 @@
     def stat_copy(step):
         other = lax.rem(me + step, devices)
         return pltpu.make_async_remote_copy(
-            src_ref=stats.at[(other * rows) // message],
+            src_ref=stats.at[lax.div(other * rows, message)],
             dst_ref=got_stats.at[me],
             send_sem=stat_send.at[step],
             recv_sem=stat_recv.at[step],
-            device_id=(other // shards, lax.rem(other, shards)),
+            device_id=(lax.div(other, shards), lax.rem(other, shards)),
             device_id_type=MESH,
         )
 
@@ -538,7 +533,6 @@
     tokens = groups * tok_grp
     rows = tok_grp // shards
     message = max(8, rows)
-    key_count = kv_pages.shape[1] * page_len
     size_x = shards // 2
 
     vmem = pl.BlockSpec(memory_space=pltpu.VMEM)
@@ -551,9 +545,8 @@
         in_specs=[vmem, vmem, hbm, vmem, vmem, smem, vmem, hbm, vmem, vmem, vmem, hbm],
         out_specs=vmem,
         scratch_shapes=[
-            pltpu.VMEM((2, 2 * key_count, flat_width), BF16),
-            pltpu.VMEM((2, key_count, flat_width), BF16),
-            pltpu.VMEM((2, key_count, flat_width), BF16),
+            pltpu.VMEM((2, kv_pages.shape[1], page_len, flat_width), BF16),
+            pltpu.VMEM((2, kv_pages.shape[1], page_len, flat_width), BF16),
             pltpu.VMEM(out_proj.shape, BF16),
             pltpu.VMEM(vocab.shape, BF16),
             pltpu.VMEM((groups, 2, tok_grp, flat_width), BF16),
@@ -568,7 +561,7 @@
             pltpu.VMEM((2, 2, devices // 2, 2 * rows, width // 2), BF16),
             pltpu.VMEM((tokens // message, message, LANES), F32),
             pltpu.VMEM((devices, message, LANES), F32),
-            dma((3,)),
+            dma((4,)),
             dma((groups,)),
             dma((groups,)),
             dma((2, groups)),
@@ -590,10 +583,10 @@
         name="rollout_logprob",
     )(
         query,
-        self_kv.reshape(2, 2 * tok_grp, flat_width),
-        kv_pages.reshape(2, 2 * key_count, flat_width),
-        page_dest,
-        page_request[None, :],
+        self_kv,
+        jnp.swapaxes(kv_pages, 2, 3),
+        jnp.transpose(page_dest),
+        page_request.reshape(-1, LANES),
         score_len,
         targets[None, :],
         out_proj,

time: 77.8 us -> 71.4 us (0.918)
  local copies, waits for them, and re-layouts: 11.3 us -> 5.62 us
    reshape x2 -> x0, local copies, waits for them, and re-layouts: 7.34 us -> none  [the longest x1 5.74 us: per_device(): kv_pages.reshape(2, 2 * key_count, flat_width)]
    unnamed x2, local copies, waits for them, and re-layouts: 2.74 us -> 5.62 us
    broadcast_in_dim x1 -> x0, local copies, waits for them, and re-layouts: 1.27 us -> none  [per_device(): page_request[None, :]]
where the time goes in v3:
time: 71.4 us; the launch traced here: 71.1 us
  Pallas kernels  65.5 us (92%)
  local copies, waits for them, and re-layouts  5.62 us (8%)
    pallas_call x1, Pallas kernels, per_device(): pl.pallas_call(functools.partial(kernel, groups, shards, page_len), out_s...  65.5 us
    unnamed x2, local copies, waits for them, and re-layouts  5.62 us

profile of v3, /device:TPU:0, one launch (start us, length us, event | category | flops | bytes accessed | tf_op | source)
XLA Modules:
  0.0 71.1 jit_solution(2365126243252484432)
XLA Ops:
  0.0 4.4 %copy.15 = bf16[2,48,16,2,512]{4,2,3,1,0:T(8,128)(2,1)} copy(bf16[2,48,16,2,512]{4,3,2,1,0:T(2,128)(2,1)} %param.14) | data formatting | bytes 6291456 | tf_op args[2]
  4.4 65.5 %rollout_logprob.1 = f32[2,8]{1,0:T(2,128)} custom-call(bf16[2,32,512]{2,1,0:T(8,128)(2,1)} %query_ref.1, bf16[2,32,2,512]{3,2,1,0:T(2,128)(2,1)} %own_ref.1, bf16[2,48,2,16,512]{4,3,2,1,0:T(8,128)(2,1)} %bitcast.6, s32[1,384]{1,0:T(1,128)} %bitcast.8, s32[3,128]{1,0:T(4,128)} %bitcast.7, s32[2]{0:T(128)} %score_len_ref.1, s32[1,256]{1,0:T(1,128)} %bitcast.9, ...), custom_call_target="tpu_custom_call" | custom-call | tf_op jit(solution)/shard_map/rollout_logprob/pallas_call | solution.py:542
  69.9 1.2 %copy.17 = f32[2,8]{1,0:T(2,128)} copy(f32[2,8]{1,0:T(2,128)} %rollout_logprob.1) | data formatting | bytes 128

commit v4 on v3

--- a/solution.py
+++ b/solution.py
@@ -258,8 +258,8 @@
         place = context * page_len + lax.rem(row, SCORE_LEN)
         allowed = token_owner == key_owner
         distance = jnp.where(allowed, (place - key_place).astype(F32), UNSEEN)
-        lane = lax.broadcasted_iota(jnp.int32, (token_count, LANES), 1)
-        packed = jnp.zeros((token_count, LANES), F32)
+        lane = lax.broadcasted_iota(jnp.int32, (size_z, 8, LANES), 2)
+        packed = jnp.zeros((size_z, 8, LANES), F32)
         for model in range(2):
             for head in range(heads):
                 span = slice(head * HEAD_DIM, (head + 1) * HEAD_DIM)
@@ -283,9 +283,13 @@
                     size_z, tok_grp, HEAD_DIM
                 )
                 column = model * heads + head
-                packed = jnp.where(lane == column, top, packed)
-                packed = jnp.where(lane == column + 64, total, packed)
-        part_stat[pl.ds(first, size_z)] = packed.reshape(size_z, tok_grp, LANES)
+                top = top.reshape(size_z, tok_grp // 8, 8, 1)
+                total = total.reshape(size_z, tok_grp // 8, 8, 1)
+                for eight in range(tok_grp // 8):
+                    at = eight * 4 * heads + column
+                    packed = jnp.where(lane == at, top[:, eight], packed)
+                    packed = jnp.where(lane == at + 2 * heads, total[:, eight], packed)
+        part_stat[pl.ds(first, size_z)] = packed
 
     loads[0].wait()
     loads[1].wait()
@@ -322,20 +326,26 @@
     for step in range(1, groups):
         sources.append((got_num, got_stat, lax.rem(my_query + step, groups)))
     source_stats = [stat[index] for _, stat, index in sources]
+
+    def stat_column(stat, column):
+        places = [eight * 4 * heads + column for eight in range(tok_grp // 8)]
+        return jnp.concatenate([stat[:, at : at + 1] for at in places], axis=0)
+
     for model in range(2):
         for head in range(heads):
             span = slice(head * HEAD_DIM, (head + 1) * HEAD_DIM)
             column = model * heads + head
             own_top, own_total, own_number = own_parts[model, head]
             top = own_top
-            for stat in source_stats:
-                top = jnp.maximum(top, stat[:, column : column + 1])
+            source_tops = [stat_column(stat, column) for stat in source_stats]
+            for source_top in source_tops:
+                top = jnp.maximum(top, source_top)
             scale = jnp.exp(own_top - top)
             total = own_total * scale
             number = own_number * scale
-            for stat, (num, _, index) in zip(source_stats, sources):
-                scale = jnp.exp(stat[:, column : column + 1] - top)
-                total = total + scale * stat[:, column + 64 : column + 65]
+            for source_top, stat, (num, _, index) in zip(source_tops, source_stats, sources):
+                scale = jnp.exp(source_top - top)
+                total = total + scale * stat_column(stat, column + 2 * heads)
                 number = number + scale * num[index, model, :, span].astype(F32)
             attended[model, :, span] = (number / total).astype(BF16)
 
@@ -551,9 +561,9 @@
             pltpu.VMEM(vocab.shape, BF16),
             pltpu.VMEM((groups, 2, tok_grp, flat_width), BF16),
             pltpu.VMEM((groups, 2, tok_grp, flat_width), BF16),
-            pltpu.VMEM((groups, tok_grp, LANES), F32),
+            pltpu.VMEM((groups, 8, LANES), F32),
             pltpu.VMEM((groups, 2, tok_grp, flat_width), BF16),
-            pltpu.VMEM((groups, tok_grp, LANES), F32),
+            pltpu.VMEM((groups, 8, LANES), F32),
             pltpu.VMEM((2, tok_grp, flat_width), BF16),
             pltpu.VMEM((2, size_x, 2 * rows, width), F32),
             pltpu.VMEM((size_x, 2 * rows, width), F32),

time: 71.4 us -> 69.4 us (0.972)
  Pallas kernels: 65.5 us -> 63.5 us
    pallas_call x1, Pallas kernels: 65.5 us -> 63.5 us  [per_device(): pl.pallas_call(functools.partial(kernel, groups, shards, page_len), out_s...]
where the time goes in v4:
time: 69.4 us; the launch traced here: 69.2 us
  Pallas kernels  63.5 us (91%)
  local copies, waits for them, and re-layouts  5.62 us (8%)
    pallas_call x1, Pallas kernels, per_device(): pl.pallas_call(functools.partial(kernel, groups, shards, page_len), out_s...  63.5 us
    unnamed x2, local copies, waits for them, and re-layouts  5.62 us

profile of v4, /device:TPU:0, one launch (start us, length us, event | category | flops | bytes accessed | tf_op | source)
XLA Modules:
  0.0 69.2 jit_solution(3650906676470798932)
XLA Ops:
  0.0 4.4 %copy.15 = bf16[2,48,16,2,512]{4,2,3,1,0:T(8,128)(2,1)} copy(bf16[2,48,16,2,512]{4,3,2,1,0:T(2,128)(2,1)} %param.14) | data formatting | bytes 6291456 | tf_op args[2]
  4.4 63.5 %rollout_logprob.1 = f32[2,8]{1,0:T(2,128)} custom-call(bf16[2,32,512]{2,1,0:T(8,128)(2,1)} %query_ref.1, bf16[2,32,2,512]{3,2,1,0:T(2,128)(2,1)} %own_ref.1, bf16[2,48,2,16,512]{4,3,2,1,0:T(8,128)(2,1)} %bitcast.6, s32[1,384]{1,0:T(1,128)} %bitcast.8, s32[3,128]{1,0:T(4,128)} %bitcast.7, s32[2]{0:T(128)} %score_len_ref.1, s32[1,256]{1,0:T(1,128)} %bitcast.9, ...), custom_call_target="tpu_custom_call" | custom-call | tf_op jit(solution)/shard_map/rollout_logprob/pallas_call | solution.py:552
  67.9 1.2 %copy.17 = f32[2,8]{1,0:T(2,128)} copy(f32[2,8]{1,0:T(2,128)} %rollout_logprob.1) | data formatting | bytes 128
